TPU v7x, 512 devices: a whole 4x8x8 slice. The times are simulated.
512 devices in a mesh: gx: 64 (over z_lo, x, y), gy: 8 (over z_hi, core).
Axes of the slice: x: 4, y: 8, z: 8 (z_hi: 4, z_lo: 2; z = z_hi * 2 + z_lo), core: 2. Of those that a mesh axis runs over, the one named last changes fastest.
Arguments:
- position: float32 [3, 2097152], P(None, ('gx', 'gy')), may hold values from 0.05 to 0.95, as said below
- momentum: float32 [3, 2097152], P(None, ('gx', 'gy')), may hold values from -1.6 to 1.6, as said below
- cell_first: int32 [3, 2097152], P(None, ('gx', 'gy')), may hold values from 0 to 255, as said below
- cell_second: int32 [3, 2097152], P(None, ('gx', 'gy')), may hold values from 0 to 255, as said below
- destination: int32 [2097152], P(('gx', 'gy')), may hold values from 0 to 4, as said below
- slot_index: int32 [2097152], P(('gx', 'gy')), may hold values from 0 to 4095, as said below
- pull_position: float32 [3, 2097152], P(None, ('gx', 'gy')), may hold values from -6 to 6
- pull_momentum: float32 [3, 2097152], P(None, ('gx', 'gy')), may hold values from -6 to 6
Outputs:
- grad_position: float32 [3, 2097152], P(None, ('gx', 'gy'))
- grad_momentum: float32 [3, 2097152], P(None, ('gx', 'gy'))
Inputs may be any that keep to these rules, and one draw needn't show every extreme that they name: `destination`: 0: the particle stays on its device; 1 and 2: it moves to the next and to the previous device along gx; 3 and 4: to the next and to the previous device along gy (both axes wrap). From the particles of one device at most 256 go to each of its four neighbours, and in every draw some device sends exactly 256 to one neighbour. Between two neighbouring devices as many particles move one way as the other. A particle that moves to the next (previous) device along an axis lies in the last (first) cell layer of its device along that axis in cell_first. Over all particles the destination device and slot_index fill every index of every device exactly once. `cell_first`: the first component is below 2, the second below 8, the third below 256. `cell_second`: the cell_first of the particle that lands at this index, moved with it: a particle moving along gx goes from the last layer to the first or from the first to the last, likewise along gy; other components stay. The first component is below 2, the second below 8, the third below 256. `position`: A particle's drift_one leaves its cell along an axis exactly where destination sends it across that axis, in that direction. `momentum`: momenta of particles that move carry them across the cell face toward their destination.
All inputs are finite; a program needn't handle non-finite values.
Results may differ from a plain program's by a relative error of at most 0.000058.
Values sent between devices are 32-bit elements; how exact they have to be, the bound alone decides.
No kernel may reach another device: no remote copies, remote signals or barrier semaphores. Data moves between devices by JAX's collectives and lax.ppermute only.
A program may use at most 64 MiB of HBM per device.

v0:
```python
import jax
import jax.numpy as jnp
from jax import lax
from jax.sharding import PartitionSpec as P

CX = 2
CY = 8
NZ = 256
MOVE_MOST = 256
highest = lax.Precision.HIGHEST
step_size = 0.25
strength = 0.02


def with_halo(x, sides, width):
    for axis, dim in sides:
        peers, length = (lax.axis_size(axis), x.shape[dim])
        up = [(i, (i + 1) % peers) for i in range(peers)]
        down = [(j, i) for i, j in up]
        last = lax.slice_in_dim(x, length - width, length, axis=dim)
        first = lax.slice_in_dim(x, 0, width, axis=dim)
        before = lax.ppermute(last, axis, up)
        after = lax.ppermute(first, axis, down)
        x = jnp.concatenate([before, x, after], axis=dim)
    return x


def kernel_block(targets, sources, extent, reach_cells):
    distance = jnp.abs(targets[:, None] - sources[None, :])
    distance = jnp.minimum(distance, extent - distance)
    return jnp.exp(-distance.astype(jnp.float32) / reach_cells)


def cloud_weights(cell_block, frac_block, plane_count, row_count, depth_cells):
    index_row = jnp.arange(row_count, dtype=jnp.int32)[:, None]
    corner = (cell_block[1] * plane_count + cell_block[0])[None, :]
    hit_base = (index_row == corner).astype(jnp.float32)
    hit_east = (index_row == corner + 1).astype(jnp.float32)
    hit_north = (index_row == corner + plane_count).astype(jnp.float32)
    hit_both = (index_row == corner + plane_count + 1).astype(jnp.float32)
    west_weight = (1.0 - frac_block[0])[None, :]
    east_weight = frac_block[0][None, :]
    south_weight = (1.0 - frac_block[1])[None, :]
    north_weight = frac_block[1][None, :]
    planar = (
        hit_base * (west_weight * south_weight)
        + hit_east * (east_weight * south_weight)
        + hit_north * (west_weight * north_weight)
        + hit_both * (east_weight * north_weight)
    )
    slope_east = (hit_east - hit_base) * south_weight + (hit_both - hit_north) * north_weight
    slope_north = (hit_north - hit_base) * west_weight + (hit_both - hit_east) * east_weight
    index_depth = jnp.arange(depth_cells, dtype=jnp.int32)[:, None]
    lower_hit = (index_depth == cell_block[2][None, :]).astype(jnp.float32)
    upper_hit = (index_depth == ((cell_block[2] + 1) % depth_cells)[None, :]).astype(jnp.float32)
    vertical = lower_hit * (1.0 - frac_block[2])[None, :] + upper_hit * frac_block[2][None, :]
    slope_up = upper_hit - lower_hit
    return (planar, slope_east, slope_north, vertical, slope_up)


def particle_blocks(values):
    particle_count = values.shape[1]
    block_width = min(512, particle_count)
    return values.reshape(values.shape[0], particle_count // block_width, block_width).transpose(
        1, 0, 2
    )


def deposit(scales, cell_ids, offsets):
    layers = scales.shape[0]
    row_count = (CY + 1) * (CX + 1)

    def add_block(running, pieces):
        cell_block, frac_block, scale_block = pieces
        weights = cloud_weights(cell_block, frac_block, CX + 1, row_count, NZ)
        spread = scale_block[:, None, :] * weights[0][None]
        return (running + jnp.einsum("crb,zb->crz", spread, weights[3], precision=highest), None)

    initial = jnp.zeros((layers, row_count, NZ), jnp.float32)
    running, unused = lax.scan(
        add_block,
        initial,
        (particle_blocks(cell_ids), particle_blocks(offsets), particle_blocks(scales)),
    )
    return running.reshape(layers, CY + 1, CX + 1, NZ)


def sample_fields(fields, cell_ids, offsets, slopes):
    layers = fields.shape[0]
    row_count = fields.shape[1] * fields.shape[2]
    flattened = fields.reshape(layers * row_count, NZ)

    def one_block(pieces):
        cell_block, frac_block = pieces
        block_width = cell_block.shape[1]
        weights = cloud_weights(cell_block, frac_block, fields.shape[2], row_count, NZ)
        columns = jnp.concatenate([weights[3], weights[4]], 1) if slopes else weights[3]
        contracted = jnp.dot(
            flattened, columns, precision=highest, preferred_element_type=jnp.float32
        )
        contracted = contracted.reshape(layers, row_count, -1)
        nearby = contracted[:, :, :block_width]
        results = [jnp.sum(nearby * weights[0][None], axis=1)]
        if slopes:
            results.append(jnp.sum(nearby * weights[1][None], axis=1))
            results.append(jnp.sum(nearby * weights[2][None], axis=1))
            results.append(jnp.sum(contracted[:, :, block_width:] * weights[0][None], axis=1))
        return jnp.stack(results, 0)

    blocked = lax.map(one_block, (particle_blocks(cell_ids), particle_blocks(offsets)))
    return blocked.transpose(1, 2, 0, 3).reshape(blocked.shape[1], layers, cell_ids.shape[1])


def fold_planes(slab):
    planes = slab.shape[2]
    widened = with_halo(slab, (("gx", 2),), 2)
    return jnp.concatenate(
        [
            widened[:, :, 0:1],
            widened[:, :, 1:2] + widened[:, :, 2:3],
            widened[:, :, 3 : planes + 1],
            widened[:, :, planes + 1 : planes + 2] + widened[:, :, planes + 2 : planes + 3],
            widened[:, :, planes + 3 : planes + 4],
        ],
        axis=2,
    )


def smooth_depth(field):
    depth_cells = field.shape[-1]
    axis_cells = jnp.arange(depth_cells, dtype=jnp.int32)
    matrix = kernel_block(axis_cells, axis_cells, depth_cells, depth_cells / 16.0)
    return jnp.dot(
        field.reshape(-1, depth_cells),
        matrix,
        precision=highest,
        preferred_element_type=jnp.float32,
    ).reshape(field.shape)


def sum_lines(field):
    members = lax.axis_size("gy")
    band_rows = field.shape[1]
    own_rows = band_rows - 1
    extent = own_rows * members
    reach_cells = extent / 4.0
    anchor = lax.axis_index("gy") * own_rows
    targets = (anchor + jnp.arange(-1, own_rows + 2, dtype=jnp.int32)) % extent
    initial = jnp.zeros((field.shape[0], own_rows + 3, field.shape[2], field.shape[3]), jnp.float32)
    gathered = lax.all_gather(field, "gy", axis=1, tiled=True)
    length = gathered.shape[1]
    positions = jnp.arange(length, dtype=jnp.int32)
    sources = (positions // band_rows * own_rows + positions % band_rows) % extent
    weights = kernel_block(targets, sources, extent, reach_cells)
    return initial + jnp.einsum("ab,cbxz->caxz", weights, gathered, precision=highest)


def force_field(density):
    potential = sum_lines(smooth_depth(fold_planes(density)))
    potential = strength * potential
    centre = potential[:, 1:-1, 1:-1]
    push_east = -0.5 * (potential[:, 1:-1, 2:] - potential[:, 1:-1, :-2])
    push_north = -0.5 * (potential[:, 2:, 1:-1] - potential[:, :-2, 1:-1])
    push_up = -0.5 * (jnp.roll(centre, -1, 3) - jnp.roll(centre, 1, 3))
    return jnp.concatenate([push_east, push_north, push_up], 0)


def force_pullback(pushes, cell_ids, offsets, pull_force):
    folded = fold_planes(deposit(pull_force, cell_ids, offsets))
    across = 0.5 * (folded[0:1, :, 2:] - folded[0:1, :, :-2])
    upward = folded[2:3, :, 1:-1]
    across = across + 0.5 * (jnp.roll(upward, -1, 3) - jnp.roll(upward, 1, 3))
    line_sums = sum_lines(jnp.concatenate([across, folded[1:2, :, 1:-1]], 0))
    summed = line_sums[0:1, 1:-1] + 0.5 * (line_sums[1:2, 2:] - line_sums[1:2, :-2])
    density_pull = strength * smooth_depth(summed)
    sampled = sample_fields(jnp.concatenate([pushes, density_pull], 0), cell_ids, offsets, True)
    slopes = sampled[1:]
    return jnp.sum(slopes[:, :3] * pull_force[None], axis=1) + slopes[:, 3]


def pack_moves(destination, capacity):
    particle_count = destination.shape[0]
    grouped = jnp.argsort(destination, stable=True)
    group_size = jnp.sum(
        (destination[None, :] == jnp.arange(5, dtype=jnp.int32)[:, None]).astype(jnp.int32), axis=1
    )
    opening = jnp.cumsum(group_size) - group_size
    lane_index = jnp.arange(capacity, dtype=jnp.int32)
    chosen = jnp.stack(
        [
            grouped[jnp.minimum(opening[move_code] + lane_index, particle_count - 1)]
            for move_code in range(1, 5)
        ],
        0,
    )
    filled = lane_index[None, :] < group_size[1:5, None]
    return (chosen, filled)


def trade_pairs(outward_x, outward_y):
    widened_x = with_halo(outward_x, (("gx", 1),), 1)
    widened_y = with_halo(outward_y, (("gy", 1),), 1)
    return (widened_x[:, 0], widened_x[:, 3], widened_y[:, 0], widened_y[:, 3])


def local(
    position,
    momentum,
    cell_first,
    cell_second,
    destination,
    slot_index,
    pull_position,
    pull_momentum,
):
    particle_count = position.shape[1]
    unit_mass = jnp.ones((1, particle_count), jnp.float32)
    drift_one = position + step_size * momentum
    push_one = force_field(deposit(unit_mass, cell_first, drift_one))
    kick_one = momentum + step_size * sample_fields(push_one, cell_first, drift_one, False)[0]
    eastward = (destination == 1).astype(jnp.float32) - (destination == 2).astype(jnp.float32)
    northward = (destination == 3).astype(jnp.float32) - (destination == 4).astype(jnp.float32)
    shift_cells = jnp.stack([eastward, northward, jnp.zeros_like(eastward)], 0)
    payload = jnp.concatenate([drift_one - shift_cells, kick_one], 0)
    chosen, filled = pack_moves(destination, MOVE_MOST)
    slot_marks = jnp.where(filled, slot_index[chosen], particle_count).astype(jnp.float32)
    parcel = jnp.where(filled[None], payload[:, chosen], 0.0)
    parcel = jnp.concatenate([parcel, slot_marks[None]], 0)
    arrivals = trade_pairs(
        jnp.stack([parcel[:, 1], parcel[:, 0]], 1), jnp.stack([parcel[:, 3], parcel[:, 2]], 1)
    )
    arrivals = jnp.concatenate(arrivals, 1)
    received = arrivals[6].astype(jnp.int32)
    staying = jnp.where(destination == 0, slot_index, particle_count)
    placed = jnp.concatenate([staying, received], 0)
    arrived = (
        jnp.zeros((6, particle_count), jnp.float32)
        .at[:, placed]
        .set(jnp.concatenate([payload, arrivals[:6]], 1), mode="drop")
    )
    drift_two = arrived[:3] + step_size * arrived[3:]
    push_two = force_field(deposit(unit_mass, cell_second, drift_two))
    grad_drift_two = pull_position + force_pullback(
        push_two, cell_second, drift_two, step_size * pull_momentum
    )
    grad_kick_two = pull_momentum + step_size * grad_drift_two
    returning = jnp.concatenate([grad_drift_two, grad_kick_two], 0)
    sent_back = jnp.where(
        received[None] < particle_count,
        returning[:, jnp.minimum(received, particle_count - 1)],
        0.0,
    )
    sent_back = sent_back.reshape(6, 4, MOVE_MOST)
    homecoming = trade_pairs(sent_back[:, 0:2], sent_back[:, 2:4])
    returned = jnp.stack([homecoming[1], homecoming[0], homecoming[3], homecoming[2]], 1)
    gathered_home = jnp.where(destination[None] == 0, returning[:, slot_index], 0.0)
    home_spots = jnp.where(filled, chosen, particle_count).reshape(-1)
    gathered_home = gathered_home.at[:, home_spots].set(returned.reshape(6, -1), mode="drop")
    grad_drift_one = gathered_home[:3] + force_pullback(
        push_one, cell_first, drift_one, step_size * gathered_home[3:]
    )
    grad_momentum = gathered_home[3:] + step_size * grad_drift_one
    return (grad_drift_one, grad_momentum)


def solution(mesh):
    return jax.shard_map(
        local,
        mesh=mesh,
        in_specs=(
            P(None, ("gx", "gy")),
            P(None, ("gx", "gy")),
            P(None, ("gx", "gy")),
            P(None, ("gx", "gy")),
            P(("gx", "gy")),
            P(("gx", "gy")),
            P(None, ("gx", "gy")),
            P(None, ("gx", "gy")),
        ),
        out_specs=(P(None, ("gx", "gy")), P(None, ("gx", "gy"))),
        check_vma=False,
    )
```

profile of v0, /device:TPU:1, one launch (start us, length us, event | category | flops | bytes accessed | tf_op | source)
XLA Modules:
  0.0 329.3 jit_solution(1960830378543347206)
XLA Ops:
  1.4 1.0 maximum_subtract_fusion
  2.4 12.2 %while.91 = (s32[]{:T(128)}, f32[1,27,256]{2,1,0:T(8,128)S(1)}, s32[8,3,512]{2,1,0:T(4,128)}, f32[8,3,512]{2,1,0:T(4,128)S(1)}, s32[]{:T(128)}, /*index=5*/s32[]{:T(128)}, s32[]{}, s32[]{}) while((s32[]{:T(128)}, f32[1,27,256]{2,1,0:T(8,128)S(1)}, s32[8,3,512]{2,1,0:T(4,128)}, f32[8,3,512]{2,1,0:T(4,128)S(1)}, s32[]{:T(128)}, ...), condition=%wide.region_2.3_spmd.clone, body=%wide.region_1.2_spmd.clone.sunk | while | flops 43300868 | bytes 131215 | solution.py:80
  2.5 0.8 dynamic-slice_add_fusion.17
  4.0 0.8 dynamic-slice_add_fusion.17
  5.5 0.8 dynamic-slice_add_fusion.17
  7.0 0.8 dynamic-slice_add_fusion.17
  8.5 0.8 dynamic-slice_add_fusion.17
  10.1 0.8 dynamic-slice_add_fusion.17
  11.6 0.8 dynamic-slice_add_fusion.17
  13.1 0.8 dynamic-slice_add_fusion.17
  14.7 4.0 %collective-permute-start = (f32[1,9,2,256]{3,1,2,0:T(8,128)S(1)}, f32[1,9,2,256]{3,1,2,0:T(8,128)S(1)}, u32[]{:S(2)}, u32[]{:S(2)}) collective-permute-start(f32[1,9,2,256]{3,1,2,0:T(8,128)S(1)} %copy.330), channel_id=1, source_target_pairs={{0,8},{8,16},{16,24},{24,32},{32,40},{40,48},{48,56},{56,64},{64,7... | collective-permute-start | bytes 55304 | tf_op jit(solution)/shard_map/ppermute | solution.py:22
  18.7 7.8 %collective-permute-start.1 = (f32[1,9,2,256]{3,1,2,0:T(8,128)S(1)}, f32[1,9,2,256]{3,1,2,0:T(8,128)S(1)}, u32[]{:S(2)}, u32[]{:S(2)}) collective-permute-start(f32[1,9,2,256]{3,1,2,0:T(8,128)S(1)} %copy.334), channel_id=1, source_target_pairs={{8,0},{16,8},{24,16},{32,24},{40,32},{48,40},{56,48},{64,56},{72,6... | collective-permute-start | bytes 55304 | tf_op jit(solution)/shard_map/ppermute | solution.py:23
  28.9 5.8 %sort.17 = (s32[4096]{0:T(1024)}, s32[4096]{0:T(1024)S(1)}) sort(s32[4096]{0:T(1024)S(1)} %copy-done.3, s32[4096]{0:T(1024)S(1)} %iota.429), dimensions={0}, to_apply=%region_6.7 | sort | flops 49152 | bytes 65536 | tf_op jit(solution)/shard_map/jit(argsort)/sort | solution.py:183
  34.7 1.7 gather_fusion
  36.4 1.7 gather_fusion.1
  39.5 1.7 gather_fusion.2
  41.2 1.7 gather_fusion.3
  43.1 6.2 %gather_fusion.5 = s32[1024]{0:T(1024)S(1)} fusion(s32[4096]{0:T(1024)S(1)} %copy-done, s32[1024]{0:T(1024)S(1)} %broadcast_clamp_fusion.1), kind=kCustom, calls=%fused_computation.5 | custom fusion | bytes 12288 | tf_op jit(solution)/shard_map/gather | solution.py:226
  49.9 20.6 %all-gather = f32[72,5,256]{2,1,0:T(8,128)S(1)} all-gather(f32[9,5,256]{2,1,0:T(8,128)S(1)} %fusion.143), channel_id=2, replica_groups=mesh['gx'=64,'gy'=8] {'gy'}, dimensions={0}, use_global_device_ids=true | all-gather | bytes 414720 | tf_op jit(solution)/shard_map/all_gather | solution.py:150
  71.4 13.0 %while.88 = (s32[]{:T(128)}, f32[8,1,3,512]{3,2,1,0:T(4,128)S(1)}, s32[8,3,512]{2,1,0:T(4,128)}, f32[8,3,512]{2,1,0:T(4,128)S(1)}, f32[81,256]{1,0:T(8,128)S(1)}, /*index=5*/s32[]{:T(128)}, s32[]{:T(128)}, s32[]{}, s32[]{}) while((s32[]{:T(128)}, f32[8,1,3,512]{3,2,1,0:T(4,128)S(1)}, s32[8,3,512]{2,1,0:T(4,128)}, f32[8,3,512]{2,1,0:T(4,128)S(1)}, ...), condition=%wide.region_5.6_spmd, body=%wide.region_3.5_spmd.sunk | while | flops 128303104 | bytes 955537 | solution.py:110
  71.4 0.8 dynamic-slice_add_fusion.14
  73.0 0.8 dynamic-slice_add_fusion.14
  76.3 0.8 dynamic-slice_add_fusion.14
  81.1 0.8 dynamic-slice_add_fusion.14
  85.1 2.8 gather_fusion.4
  88.1 2.1 collective-permute-start.5
  90.2 4.4 %collective-permute-start.4 = (f32[7,1,256]{2,1,0:T(1,128)S(1)}, f32[7,1,256]{2,1,0:T(1,128)S(1)}, u32[]{:S(2)}, u32[]{:S(2)}) collective-permute-start(f32[7,1,256]{2,1,0:T(1,128)S(1)} %get-tuple-element.759), channel_id=1, source_target_pairs={{0,1},{1,2},{2,3},{3,4},{4,5},{5,6},{6,7},{7,0},{8,9},{9,10},{10,1... | collective-permute-start | bytes 21512 | tf_op jit(solution)/shard_map/ppermute | solution.py:22
  94.6 4.4 %collective-permute-start.3 = (f32[7,1,256]{2,1,0:T(1,128)S(1)}, f32[7,1,256]{2,1,0:T(1,128)S(1)}, u32[]{:S(2)}, u32[]{:S(2)}) collective-permute-start(f32[7,1,256]{2,1,0:T(1,128)S(1)} %get-tuple-element.757), channel_id=1, source_target_pairs={{8,0},{16,8},{24,16},{32,24},{40,32},{48,40},{56,48},{64,56},{72,6... | collective-permute-start | bytes 21512 | tf_op jit(solution)/shard_map/ppermute | solution.py:23
  99.0 1.9 collective-permute-start.2
  101.0 6.6 %collective-permute-done.2 = f32[7,1,256]{2,1,0:T(1,128)S(1)} collective-permute-done((f32[7,1,256]{2,1,0:T(1,128)S(1)}, f32[7,1,256]{2,1,0:T(1,128)S(1)}, u32[]{:S(2)}, u32[]{:S(2)}) %collective-permute-start.2) | collective-permute-done | bytes 7200 | tf_op jit(solution)/shard_map/ppermute | solution.py:22
  107.7 2.2 copy.281
  109.9 14.1 %scatter_custom_fusion = f32[6,4096]{0,1:T(8,128)S(1)} fusion(s32[5120]{0:T(1024)S(1)} %bitcast.439, f32[5120,6]{1,0:T(8,128)} %copy.281, f32[]{:T(128)} %constant.571.clone.1), kind=kCustom, calls=%fused_computation.335 | custom fusion | bytes 98816 | tf_op jit(solution)/shard_map/scatter | solution.py:239
  124.0 2.6 fusion.253
  126.6 2.4 copy.335
  129.7 12.2 %while.92 = (s32[]{:T(128)}, f32[1,27,256]{2,1,0:T(8,128)S(1)}, s32[8,3,512]{2,1,0:T(4,128)}, f32[8,3,512]{2,1,0:T(4,128)S(1)}, s32[]{:T(128)}, /*index=5*/s32[]{:T(128)}, s32[]{}, s32[]{}) while((s32[]{:T(128)}, f32[1,27,256]{2,1,0:T(8,128)S(1)}, s32[8,3,512]{2,1,0:T(4,128)}, f32[8,3,512]{2,1,0:T(4,128)S(1)}, s32[]{:T(128)}, ...), condition=%wide.region_10.11_spmd.clone, body=%wide.region_9.10_spmd.clone.sunk | while | flops 43300868 | bytes 131215 | solution.py:80
  129.7 0.8 dynamic-slice_add_fusion.18
  131.2 0.8 dynamic-slice_add_fusion.18
  132.8 0.8 dynamic-slice_add_fusion.18
  134.3 0.8 dynamic-slice_add_fusion.18
  141.9 13.4 %while.93 = (s32[]{:T(128)}, f32[3,27,256]{2,1,0:T(8,128)S(1)}, f32[8,3,512]{2,1,0:T(4,128)S(1)}, s32[8,3,512]{2,1,0:T(4,128)}, f32[8,3,512]{2,1,0:T(4,128)S(1)}, /*index=5*/s32[]{:T(128)}, s32[]{:T(128)}, s32[]{}, s32[]{}) while((s32[]{:T(128)}, f32[3,27,256]{2,1,0:T(8,128)S(1)}, f32[8,3,512]{2,1,0:T(4,128)S(1)}, ...), condition=%wide.region_12.13_spmd.clone, body=%wide.region_11.12_spmd.clone.sunk | while | flops 128304640 | bytes 370843 | solution.py:80
  155.5 1.9 collective-permute-start.6
  157.4 7.6 %collective-permute-start.7 = (f32[1,9,2,256]{3,1,2,0:T(8,128)S(1)}, f32[1,9,2,256]{3,1,2,0:T(8,128)S(1)}, u32[]{:S(2)}, u32[]{:S(2)}) collective-permute-start(f32[1,9,2,256]{3,1,2,0:T(8,128)S(1)} %copy.341), channel_id=1, source_target_pairs={{8,0},{16,8},{24,16},{32,24},{40,32},{48,40},{56,48},{64,56},{72,6... | collective-permute-start | bytes 55304 | tf_op jit(solution)/shard_map/ppermute | solution.py:23
  165.0 1.9 collective-permute-start.9
  167.0 7.6 %collective-permute-start.8 = (f32[3,9,2,256]{3,1,2,0:T(8,128)S(1)}, f32[3,9,2,256]{3,1,2,0:T(8,128)S(1)}, u32[]{:S(2)}, u32[]{:S(2)}) collective-permute-start(f32[3,9,2,256]{3,1,2,0:T(8,128)S(1)} %copy.344), channel_id=1, source_target_pairs={{8,0},{16,8},{24,16},{32,24},{40,32},{48,40},{56,48},{64,56},{72,6... | collective-permute-start | bytes 165896 | tf_op jit(solution)/shard_map/ppermute | solution.py:23
  175.1 18.5 %all-gather.1 = f32[72,5,256]{2,1,0:T(8,128)S(1)} all-gather(f32[9,5,256]{2,1,0:T(8,128)S(1)} %fusion.141), channel_id=3, replica_groups=mesh['gx'=64,'gy'=8] {'gy'}, dimensions={0}, use_global_device_ids=true | all-gather | bytes 414720 | tf_op jit(solution)/shard_map/all_gather | solution.py:150
  194.6 14.8 %all_gather.14 = f32[2,72,3,256]{3,0,2,1:T(2,128)S(1)} all-gather(f32[2,9,3,256]{3,0,2,1:T(2,128)S(1)} %copy.298), channel_id=1, replica_groups=mesh['gx'=64,'gy'=8] {'gy'}, dimensions={1}, use_global_device_ids=true | all-gather | bytes 497664 | tf_op jit(solution)/shard_map/all_gather | solution.py:150
  210.4 16.8 %while.89 = (s32[]{:T(128)}, f32[8,4,4,512]{3,2,1,0:T(4,128)S(1)}, s32[8,3,512]{2,1,0:T(4,128)}, f32[8,3,512]{2,1,0:T(4,128)S(1)}, f32[108,256]{1,0:T(8,128)S(1)}, /*index=5*/s32[]{:T(128)}, s32[]{:T(128)}, s32[]{}, s32[]{}) while((s32[]{:T(128)}, f32[8,4,4,512]{3,2,1,0:T(4,128)S(1)}, s32[8,3,512]{2,1,0:T(4,128)}, ...), condition=%wide.region_18.19_spmd, body=%wide.region_13.18_spmd.sunk | while | flops 341865984 | bytes 4495505 | solution.py:110
  228.2 2.8 gather_fusion.7
  231.3 2.3 collective-permute-start.10
  233.6 3.0 collective-permute-start.11
  236.6 2.6 collective-permute-start.12
  239.2 3.8 %collective-permute-start.13 = (f32[6,1,256]{2,1,0:T(1,128)S(1)}, f32[6,1,256]{2,1,0:T(1,128)S(1)}, u32[]{:S(2)}, u32[]{:S(2)}) collective-permute-start(f32[6,1,256]{2,1,0:T(1,128)S(1)} %get-tuple-element.771), channel_id=1, source_target_pairs={{0,1},{1,2},{2,3},{3,4},{4,5},{5,6},{6,7},{7,0},{8,9},{9,10},{10,1... | collective-permute-start | bytes 18440 | tf_op jit(solution)/shard_map/ppermute | solution.py:22
  243.0 14.1 %gather_fusion.6 = f32[4096,6]{1,0:T(8,128)} fusion(f32[6,4096]{0,1:T(8,128)S(1)} %copy.303, s32[4096]{0:T(1024)S(1)} %get-tuple-element.774), kind=kCustom, calls=%fused_computation.6 | custom fusion | bytes 212992 | tf_op jit(solution)/shard_map/gather | solution.py:256
  257.1 3.6 %select_bitcast_fusion = f32[6,4096]{0,1:T(8,128)S(1)} fusion(f32[4096,6]{1,0:T(8,128)} %gather_fusion.6, pred[4096]{0:T(1024)(128)(4,1)S(1)} %get-tuple-element.613), kind=kLoop, calls=%fused_computation.324 | loop fusion | flops 24576 | bytes 200704 | tf_op jit(solution)/shard_map/jit(_where)/select_n | solution.py:256
  261.0 4.1 %scatter_fusion = f32[6,4096]{0,1:T(8,128)S(1)} fusion(f32[6,4096]{0,1:T(8,128)S(1)} %select_bitcast_fusion, s32[1024]{0:T(1024)S(1)} %bitcast.440, f32[1024,6]{1,0:T(8,128)S(1)} %bitcast.355), kind=kCustom, calls=%fused_computation.9 | custom fusion | bytes 77824 | tf_op jit(solution)/shard_map/scatter | solution.py:258
  265.1 2.7 fusion.252
  267.8 2.2 copy.349
  270.1 13.4 %while.94 = (s32[]{:T(128)}, f32[3,27,256]{2,1,0:T(8,128)S(1)}, f32[8,3,512]{2,1,0:T(4,128)S(1)}, s32[8,3,512]{2,1,0:T(4,128)}, f32[8,3,512]{2,1,0:T(4,128)S(1)}, /*index=5*/s32[]{:T(128)}, s32[]{:T(128)}, s32[]{}, s32[]{}) while((s32[]{:T(128)}, f32[3,27,256]{2,1,0:T(8,128)S(1)}, f32[8,3,512]{2,1,0:T(4,128)S(1)}, ...), condition=%wide.region_22.23_spmd.clone, body=%wide.region_21.22_spmd.clone.sunk | while | flops 128304640 | bytes 370843 | solution.py:80
  270.1 0.9 dynamic-slice_add_fusion.20
  283.6 1.9 collective-permute-start.15
  285.6 7.6 %collective-permute-start.14 = (f32[3,9,2,256]{3,1,2,0:T(8,128)S(1)}, f32[3,9,2,256]{3,1,2,0:T(8,128)S(1)}, u32[]{:S(2)}, u32[]{:S(2)}) collective-permute-start(f32[3,9,2,256]{3,1,2,0:T(8,128)S(1)} %copy.352), channel_id=1, source_target_pairs={{8,0},{16,8},{24,16},{32,24},{40,32},{48,40},{56,48},{64,56},{72,6... | collective-permute-start | bytes 165896 | tf_op jit(solution)/shard_map/ppermute | solution.py:23
  294.3 1.2 collective-permute-done.14
  295.7 14.8 %all_gather.15 = f32[2,72,3,256]{3,0,2,1:T(2,128)S(1)} all-gather(f32[2,9,3,256]{3,0,2,1:T(2,128)S(1)} %copy.315), channel_id=1, replica_groups=mesh['gx'=64,'gy'=8] {'gy'}, dimensions={1}, use_global_device_ids=true | all-gather | bytes 497664 | tf_op jit(solution)/shard_map/all_gather | solution.py:150
  311.5 16.8 %while.90 = (s32[]{:T(128)}, f32[8,4,4,512]{3,2,1,0:T(4,128)S(1)}, s32[8,3,512]{2,1,0:T(4,128)}, f32[8,3,512]{2,1,0:T(4,128)S(1)}, f32[108,256]{1,0:T(8,128)S(1)}, /*index=5*/s32[]{:T(128)}, s32[]{:T(128)}, s32[]{}, s32[]{}) while((s32[]{:T(128)}, f32[8,4,4,512]{3,2,1,0:T(4,128)S(1)}, s32[8,3,512]{2,1,0:T(4,128)}, ...), condition=%wide.region_28.29_spmd, body=%wide.region_23.28_spmd.sunk | while | flops 341865984 | bytes 4495505 | solution.py:110
  (658 shorter events, 94.8 us)
Async XLA Ops:
  2.4 24.2 %copy-start.3 = (s32[4096]{0:T(1024)S(1)}, s32[4096]{0:T(1024)}, u32[]{:S(2)}) copy-start(s32[4096]{0:T(1024)} %param.26) | copy-start | bytes 49156
  14.7 34.8 %collective-permute-start = (f32[1,9,2,256]{3,1,2,0:T(8,128)S(1)}, f32[1,9,2,256]{3,1,2,0:T(8,128)S(1)}, u32[]{:S(2)}, u32[]{:S(2)}) collective-permute-start(f32[1,9,2,256]{3,1,2,0:T(8,128)S(1)} %copy.330), channel_id=1, source_target_pairs={{0,8},{8,16},{16,24},{24,32},{32,40},{40,48},{48,56},{56,64},{64,7... | collective-permute-start | bytes 55304 | tf_op jit(solution)/shard_map/ppermute | solution.py:22
  18.7 30.8 %collective-permute-start.1 = (f32[1,9,2,256]{3,1,2,0:T(8,128)S(1)}, f32[1,9,2,256]{3,1,2,0:T(8,128)S(1)}, u32[]{:S(2)}, u32[]{:S(2)}) collective-permute-start(f32[1,9,2,256]{3,1,2,0:T(8,128)S(1)} %copy.334), channel_id=1, source_target_pairs={{8,0},{16,8},{24,16},{32,24},{40,32},{48,40},{56,48},{64,56},{72,6... | collective-permute-start | bytes 55304 | tf_op jit(solution)/shard_map/ppermute | solution.py:23
  34.7 8.3 %copy-start = (s32[4096]{0:T(1024)S(1)}, s32[4096]{0:T(1024)}, u32[]{:S(2)}) copy-start(s32[4096]{0:T(1024)} %param.27) | copy-start | bytes 49156
  43.1 6.3 %copy-start.5 = (f32[3,4096]{1,0:T(4,128)S(1)}, f32[3,4096]{1,0:T(4,128)}, u32[]{:S(2)}) copy-start(f32[3,4096]{1,0:T(4,128)} %param.29) | copy-start | bytes 147460
  71.3 13.0 %copy-start.4 = (f32[3,4096]{1,0:T(4,128)S(1)}, f32[3,4096]{1,0:T(4,128)}, u32[]{:S(2)}) copy-start(f32[3,4096]{1,0:T(4,128)} %param.23) | copy-start | bytes 147460
  88.1 12.8 %collective-permute-start.5 = (f32[7,1,256]{2,1,0:T(1,128)S(1)}, f32[7,1,256]{2,1,0:T(1,128)S(1)}, u32[]{:S(2)}, u32[]{:S(2)}) collective-permute-start(f32[7,1,256]{2,1,0:T(1,128)S(1)} %get-tuple-element.758), channel_id=1, source_target_pairs={{1,0},{2,1},{3,2},{4,3},{5,4},{6,5},{7,6},{0,7},{9,8},{10,9},{11,1... | collective-permute-start | bytes 21512 | tf_op jit(solution)/shard_map/ppermute | solution.py:23
  90.2 10.8 %collective-permute-start.4 = (f32[7,1,256]{2,1,0:T(1,128)S(1)}, f32[7,1,256]{2,1,0:T(1,128)S(1)}, u32[]{:S(2)}, u32[]{:S(2)}) collective-permute-start(f32[7,1,256]{2,1,0:T(1,128)S(1)} %get-tuple-element.759), channel_id=1, source_target_pairs={{0,1},{1,2},{2,3},{3,4},{4,5},{5,6},{6,7},{7,0},{8,9},{9,10},{10,1... | collective-permute-start | bytes 21512 | tf_op jit(solution)/shard_map/ppermute | solution.py:22
  94.6 6.4 %collective-permute-start.3 = (f32[7,1,256]{2,1,0:T(1,128)S(1)}, f32[7,1,256]{2,1,0:T(1,128)S(1)}, u32[]{:S(2)}, u32[]{:S(2)}) collective-permute-start(f32[7,1,256]{2,1,0:T(1,128)S(1)} %get-tuple-element.757), channel_id=1, source_target_pairs={{8,0},{16,8},{24,16},{32,24},{40,32},{48,40},{56,48},{64,56},{72,6... | collective-permute-start | bytes 21512 | tf_op jit(solution)/shard_map/ppermute | solution.py:23
  99.0 8.6 %collective-permute-start.2 = (f32[7,1,256]{2,1,0:T(1,128)S(1)}, f32[7,1,256]{2,1,0:T(1,128)S(1)}, u32[]{:S(2)}, u32[]{:S(2)}) collective-permute-start(f32[7,1,256]{2,1,0:T(1,128)S(1)} %get-tuple-element.756), channel_id=1, source_target_pairs={{0,8},{8,16},{16,24},{24,32},{32,40},{40,48},{48,56},{56,64},{64,7... | collective-permute-start | bytes 21512 | tf_op jit(solution)/shard_map/ppermute | solution.py:22
  126.6 2.4 copy-start.2
  155.5 19.1 %collective-permute-start.6 = (f32[1,9,2,256]{3,1,2,0:T(8,128)S(1)}, f32[1,9,2,256]{3,1,2,0:T(8,128)S(1)}, u32[]{:S(2)}, u32[]{:S(2)}) collective-permute-start(f32[1,9,2,256]{3,1,2,0:T(8,128)S(1)} %copy.337), channel_id=1, source_target_pairs={{0,8},{8,16},{16,24},{24,32},{32,40},{40,48},{48,56},{56,64},{64,7... | collective-permute-start | bytes 55304 | tf_op jit(solution)/shard_map/ppermute | solution.py:22
  157.4 17.2 %collective-permute-start.7 = (f32[1,9,2,256]{3,1,2,0:T(8,128)S(1)}, f32[1,9,2,256]{3,1,2,0:T(8,128)S(1)}, u32[]{:S(2)}, u32[]{:S(2)}) collective-permute-start(f32[1,9,2,256]{3,1,2,0:T(8,128)S(1)} %copy.341), channel_id=1, source_target_pairs={{8,0},{16,8},{24,16},{32,24},{40,32},{48,40},{56,48},{64,56},{72,6... | collective-permute-start | bytes 55304 | tf_op jit(solution)/shard_map/ppermute | solution.py:23
  165.0 29.2 %collective-permute-start.9 = (f32[3,9,2,256]{3,1,2,0:T(8,128)S(1)}, f32[3,9,2,256]{3,1,2,0:T(8,128)S(1)}, u32[]{:S(2)}, u32[]{:S(2)}) collective-permute-start(f32[3,9,2,256]{3,1,2,0:T(8,128)S(1)} %copy.345), channel_id=1, source_target_pairs={{0,8},{8,16},{16,24},{24,32},{32,40},{40,48},{48,56},{56,64},{64,7... | collective-permute-start | bytes 165896 | tf_op jit(solution)/shard_map/ppermute | solution.py:22
  167.0 27.3 %collective-permute-start.8 = (f32[3,9,2,256]{3,1,2,0:T(8,128)S(1)}, f32[3,9,2,256]{3,1,2,0:T(8,128)S(1)}, u32[]{:S(2)}, u32[]{:S(2)}) collective-permute-start(f32[3,9,2,256]{3,1,2,0:T(8,128)S(1)} %copy.344), channel_id=1, source_target_pairs={{8,0},{16,8},{24,16},{32,24},{40,32},{48,40},{56,48},{64,56},{72,6... | collective-permute-start | bytes 165896 | tf_op jit(solution)/shard_map/ppermute | solution.py:23
  210.4 17.1 %copy-start.6 = (f32[3,4096]{1,0:T(4,128)S(1)}, f32[3,4096]{1,0:T(4,128)}, u32[]{:S(2)}) copy-start(f32[3,4096]{1,0:T(4,128)} %param.28) | copy-start | bytes 147460
  231.3 29.5 %collective-permute-start.10 = (f32[6,1,256]{2,1,0:T(1,128)S(1)}, f32[6,1,256]{2,1,0:T(1,128)S(1)}, u32[]{:S(2)}, u32[]{:S(2)}) collective-permute-start(f32[6,1,256]{2,1,0:T(1,128)S(1)} %get-tuple-element.770), channel_id=1, source_target_pairs={{8,0},{16,8},{24,16},{32,24},{40,32},{48,40},{56,48},{64,56},{72,6... | collective-permute-start | bytes 18440 | tf_op jit(solution)/shard_map/ppermute | solution.py:23
  233.6 27.1 %collective-permute-start.11 = (f32[6,1,256]{2,1,0:T(1,128)S(1)}, f32[6,1,256]{2,1,0:T(1,128)S(1)}, u32[]{:S(2)}, u32[]{:S(2)}) collective-permute-start(f32[6,1,256]{2,1,0:T(1,128)S(1)} %get-tuple-element.773), channel_id=1, source_target_pairs={{0,8},{8,16},{16,24},{24,32},{32,40},{40,48},{48,56},{56,64},{64,7... | collective-permute-start | bytes 18440 | tf_op jit(solution)/shard_map/ppermute | solution.py:22
  236.6 24.2 %collective-permute-start.12 = (f32[6,1,256]{2,1,0:T(1,128)S(1)}, f32[6,1,256]{2,1,0:T(1,128)S(1)}, u32[]{:S(2)}, u32[]{:S(2)}) collective-permute-start(f32[6,1,256]{2,1,0:T(1,128)S(1)} %get-tuple-element.772), channel_id=1, source_target_pairs={{1,0},{2,1},{3,2},{4,3},{5,4},{6,5},{7,6},{0,7},{9,8},{10,9},{11,1... | collective-permute-start | bytes 18440 | tf_op jit(solution)/shard_map/ppermute | solution.py:23
  239.2 21.6 %collective-permute-start.13 = (f32[6,1,256]{2,1,0:T(1,128)S(1)}, f32[6,1,256]{2,1,0:T(1,128)S(1)}, u32[]{:S(2)}, u32[]{:S(2)}) collective-permute-start(f32[6,1,256]{2,1,0:T(1,128)S(1)} %get-tuple-element.771), channel_id=1, source_target_pairs={{0,1},{1,2},{2,3},{3,4},{4,5},{5,6},{6,7},{7,0},{8,9},{9,10},{10,1... | collective-permute-start | bytes 18440 | tf_op jit(solution)/shard_map/ppermute | solution.py:22
  270.1 23.1 %copy-start.1 = (f32[3,4096]{0,1:T(8,128)S(1)}, f32[3,4096]{0,1:T(8,128)}, u32[]{:S(2)}) copy-start(f32[3,4096]{0,1:T(8,128)} %get-tuple-element.718) | copy-start | bytes 147460
  283.6 10.7 %collective-permute-start.15 = (f32[3,9,2,256]{3,1,2,0:T(8,128)S(1)}, f32[3,9,2,256]{3,1,2,0:T(8,128)S(1)}, u32[]{:S(2)}, u32[]{:S(2)}) collective-permute-start(f32[3,9,2,256]{3,1,2,0:T(8,128)S(1)} %copy.353), channel_id=1, source_target_pairs={{0,8},{8,16},{16,24},{24,32},{32,40},{40,48},{48,56},{56,64},{64,7... | collective-permute-start | bytes 165896 | tf_op jit(solution)/shard_map/ppermute | solution.py:22
  285.6 9.9 %collective-permute-start.14 = (f32[3,9,2,256]{3,1,2,0:T(8,128)S(1)}, f32[3,9,2,256]{3,1,2,0:T(8,128)S(1)}, u32[]{:S(2)}, u32[]{:S(2)}) collective-permute-start(f32[3,9,2,256]{3,1,2,0:T(8,128)S(1)} %copy.352), channel_id=1, source_target_pairs={{8,0},{16,8},{24,16},{32,24},{40,32},{48,40},{56,48},{64,56},{72,6... | collective-permute-start | bytes 165896 | tf_op jit(solution)/shard_map/ppermute | solution.py:23
where the time goes:
time: 334 us; the launch traced here: 329 us
  other arithmetic  71.2 us (21%)
  local copies, waits for them, and re-layouts  70.9 us (21%)
  blocking collectives  68.8 us (21%)
  starting transfers between devices  64.9 us (19%)
  matrix products  39.7 us (12%)
  waiting for transfers between devices  8.22 us (2%)
  loops' own time  3.7 us (1%)
    all_gather x4, blocking collectives, sum_lines(): gathered = lax.all_gather(field, 'gy', axis=1, tiled=True)  68.8 us
    add x56, other arithmetic, cloud_weights(): corner = (cell_block[1] * plane_count + cell_block[0])[None, :]  46.3 us
    ppermute x8, starting transfers between devices, with_halo(): after = lax.ppermute(first, axis, down)  42 us
    ppermute x8, starting transfers between devices, with_halo(): before = lax.ppermute(last, axis, up)  22.9 us
    dot_general x32, matrix products, add_block(): jnp.einsum('crb,zb->crz', spread, weights[3], precision=highest)  20.9 us
    dot_general x24, matrix products, one_block(): jnp.dot(flattened, columns, precision=highest, preferred_element_type=jnp...  15.9 us
    scatter x1, local copies, waits for them, and re-layouts, local(): arrived = jnp.zeros((6, particle_count), jnp.float32).at[:, placed].set(j...  14.1 us
    gather x1, local copies, waits for them, and re-layouts, local(): returning[:, slot_index]  14.1 us
  transfers between devices with their start and end apart: 16, of which 3 were waited for; matrix products, arithmetic and copies ran while one was open for 13% of the time, Pallas kernels for 0%

commit v1 on v0

--- a/solution.py
+++ b/solution.py
@@ -147,7 +147,9 @@
     anchor = lax.axis_index("gy") * own_rows
     targets = (anchor + jnp.arange(-1, own_rows + 2, dtype=jnp.int32)) % extent
     initial = jnp.zeros((field.shape[0], own_rows + 3, field.shape[2], field.shape[3]), jnp.float32)
-    gathered = lax.all_gather(field, "gy", axis=1, tiled=True)
+    gathered = jnp.concatenate(
+        lax.all_to_all(jnp.stack([field] * lax.axis_size("gy")), "gy", 0, 0), axis=1
+    )
     length = gathered.shape[1]
     positions = jnp.arange(length, dtype=jnp.int32)
     sources = (positions // band_rows * own_rows + positions % band_rows) % extent

time: 334 us -> 349 us (1.045)
  the two profiles are of different devices: /device:TPU:1 before, /device:TPU:62 now
where the time goes in v1:
time: 349 us; the launch traced here: 344 us
  starting transfers between devices  81.7 us (23%)
  local copies, waits for them, and re-layouts  74.8 us (21%)
  waiting for transfers between devices  71.3 us (20%)
  other arithmetic  71.2 us (20%)
  matrix products  39.8 us (11%)
  loops' own time  3.7 us (1%)
    all_to_all x4, waiting for transfers between devices, sum_lines(): lax.all_to_all(jnp.stack([field] * lax.axis_size('gy')), 'gy', 0, 0)  54.8 us
    add x56, other arithmetic, cloud_weights(): corner = (cell_block[1] * plane_count + cell_block[0])[None, :]  46.2 us
    ppermute x8, starting transfers between devices, with_halo(): before = lax.ppermute(last, axis, up)  43.8 us
    dot_general x32, matrix products, add_block(): jnp.einsum('crb,zb->crz', spread, weights[3], precision=highest)  20.9 us
    all_to_all x4, starting transfers between devices, sum_lines(): lax.all_to_all(jnp.stack([field] * lax.axis_size('gy')), 'gy', 0, 0)  20.7 us
    ppermute x8, starting transfers between devices, with_halo(): after = lax.ppermute(first, axis, down)  17.2 us
    dot_general x24, matrix products, one_block(): jnp.dot(flattened, columns, precision=highest, preferred_element_type=jnp...  15.9 us
    ppermute x8, waiting for transfers between devices, with_halo(): after = lax.ppermute(first, axis, down)  14.2 us
  transfers between devices with their start and end apart: 20, of which 8 were waited for; matrix products, arithmetic and copies ran while one was open for 13% of the time, Pallas kernels for 0%

profile of v1, /device:TPU:62, one launch (start us, length us, event | category | flops | bytes accessed | tf_op | source)
XLA Modules:
  0.0 344.3 jit_solution(6864580903838198963)
XLA Ops:
  1.4 1.0 maximum_subtract_fusion
  2.4 12.2 %while.91 = (s32[]{:T(128)}, f32[1,27,256]{2,1,0:T(8,128)S(1)}, s32[8,3,512]{2,1,0:T(4,128)}, f32[8,3,512]{2,1,0:T(4,128)S(1)}, s32[]{:T(128)}, /*index=5*/s32[]{:T(128)}, s32[]{}, s32[]{}) while((s32[]{:T(128)}, f32[1,27,256]{2,1,0:T(8,128)S(1)}, s32[8,3,512]{2,1,0:T(4,128)}, f32[8,3,512]{2,1,0:T(4,128)S(1)}, s32[]{:T(128)}, ...), condition=%wide.region_2.3_spmd.clone, body=%wide.region_1.2_spmd.clone.sunk | while | flops 43300868 | bytes 131215 | solution.py:80
  2.5 0.8 dynamic-slice_add_fusion.17
  14.6 3.4 collective-permute-start
  18.0 2.4 collective-permute-start.1
  22.3 5.8 %sort.17 = (s32[4096]{0:T(1024)}, s32[4096]{0:T(1024)S(1)}) sort(s32[4096]{0:T(1024)S(1)} %copy-done.3, s32[4096]{0:T(1024)S(1)} %iota.429), dimensions={0}, to_apply=%region_6.7 | sort | flops 49152 | bytes 65536 | tf_op jit(solution)/shard_map/jit(argsort)/sort | solution.py:185
  28.7 1.7 gather_fusion
  30.4 1.7 gather_fusion.1
  32.8 1.7 gather_fusion.2
  35.2 1.7 gather_fusion.3
  37.1 6.2 %gather_fusion.5 = s32[1024]{0:T(1024)S(1)} fusion(s32[4096]{0:T(1024)S(1)} %copy-done, s32[1024]{0:T(1024)S(1)} %broadcast_clamp_fusion.1), kind=kCustom, calls=%fused_computation.5 | custom fusion | bytes 12288 | tf_op jit(solution)/shard_map/gather | solution.py:228
  44.0 0.9 stack.129
  44.9 10.3 %all-to-all-start = ((f32[8,1,9,5,256]{4,1,3,2,0:T(1,128)}), f32[8,1,9,5,256]{4,1,3,2,0:T(1,128)S(1)}, u32[]{:S(2)}, u32[]{:S(2)}) async-start(f32[8,1,9,5,256]{4,1,3,2,0:T(1,128)} %stack.129), calls=%async_computation | async-start | bytes 737280 | tf_op jit(solution)/shard_map/all_to_all | solution.py:151
  55.2 15.0 %all-to-all-done = f32[8,1,9,5,256]{4,1,3,2,0:T(1,128)S(1)} async-done(((f32[8,1,9,5,256]{4,1,3,2,0:T(1,128)}), f32[8,1,9,5,256]{4,1,3,2,0:T(1,128)S(1)}, u32[]{:S(2)}, u32[]{:S(2)}) %all-to-all-start) | async-done | bytes 368672 | tf_op jit(solution)/shard_map/all_to_all | solution.py:151
  71.1 13.0 %while.88 = (s32[]{:T(128)}, f32[8,1,3,512]{3,2,1,0:T(4,128)S(1)}, s32[8,3,512]{2,1,0:T(4,128)}, f32[8,3,512]{2,1,0:T(4,128)S(1)}, f32[81,256]{1,0:T(8,128)S(1)}, /*index=5*/s32[]{:T(128)}, s32[]{:T(128)}, s32[]{}, s32[]{}) while((s32[]{:T(128)}, f32[8,1,3,512]{3,2,1,0:T(4,128)S(1)}, s32[8,3,512]{2,1,0:T(4,128)}, f32[8,3,512]{2,1,0:T(4,128)S(1)}, ...), condition=%wide.region_5.6_spmd, body=%wide.region_3.5_spmd.sunk | while | flops 128303104 | bytes 955537 | solution.py:110
  77.7 0.8 dynamic-slice_add_fusion.14
  79.3 0.8 dynamic-slice_add_fusion.14
  80.9 0.8 dynamic-slice_add_fusion.14
  82.5 0.8 dynamic-slice_add_fusion.14
  84.8 2.8 gather_fusion.4
  87.9 1.9 collective-permute-start.5
  89.8 2.4 collective-permute-start.4
  92.2 3.3 collective-permute-start.3
  95.5 6.8 %collective-permute-start.2 = (f32[7,1,256]{2,1,0:T(1,128)S(1)}, f32[7,1,256]{2,1,0:T(1,128)S(1)}, u32[]{:S(2)}, u32[]{:S(2)}) collective-permute-start(f32[7,1,256]{2,1,0:T(1,128)S(1)} %get-tuple-element.766), channel_id=1, source_target_pairs={{0,8},{8,16},{16,24},{24,32},{32,40},{40,48},{48,56},{56,64},{64,7... | collective-permute-start | bytes 21512 | tf_op jit(solution)/shard_map/ppermute | solution.py:22
  102.4 1.2 collective-permute-done.2
  103.7 2.3 copy.298
  106.0 14.1 %scatter_custom_fusion = f32[6,4096]{0,1:T(8,128)S(1)} fusion(s32[5120]{0:T(1024)S(1)} %bitcast.455, f32[5120,6]{1,0:T(8,128)} %copy.298, f32[]{:T(128)} %constant.571.clone.1), kind=kCustom, calls=%fused_computation.335 | custom fusion | bytes 98816 | tf_op jit(solution)/shard_map/scatter | solution.py:241
  120.1 2.6 fusion.253
  122.7 2.4 copy.346
  125.7 13.3 %while.93 = (s32[]{:T(128)}, f32[3,27,256]{2,1,0:T(8,128)S(1)}, f32[8,3,512]{2,1,0:T(4,128)S(1)}, s32[8,3,512]{2,1,0:T(4,128)}, f32[8,3,512]{2,1,0:T(4,128)S(1)}, /*index=5*/s32[]{:T(128)}, s32[]{:T(128)}, s32[]{}, s32[]{}) while((s32[]{:T(128)}, f32[3,27,256]{2,1,0:T(8,128)S(1)}, f32[8,3,512]{2,1,0:T(4,128)S(1)}, ...), condition=%wide.region_12.13_spmd.clone, body=%wide.region_11.12_spmd.clone.sunk | while | flops 128304640 | bytes 370843 | solution.py:80
  125.8 0.8 dynamic-slice_add_fusion.19
  127.5 0.8 dynamic-slice_add_fusion.19
  139.3 12.2 %while.92 = (s32[]{:T(128)}, f32[1,27,256]{2,1,0:T(8,128)S(1)}, s32[8,3,512]{2,1,0:T(4,128)}, f32[8,3,512]{2,1,0:T(4,128)S(1)}, s32[]{:T(128)}, /*index=5*/s32[]{:T(128)}, s32[]{}, s32[]{}) while((s32[]{:T(128)}, f32[1,27,256]{2,1,0:T(8,128)S(1)}, s32[8,3,512]{2,1,0:T(4,128)}, f32[8,3,512]{2,1,0:T(4,128)S(1)}, s32[]{:T(128)}, ...), condition=%wide.region_10.11_spmd.clone, body=%wide.region_9.10_spmd.clone.sunk | while | flops 43300868 | bytes 131215 | solution.py:80
  151.5 8.4 %collective-permute-start.6 = (f32[1,9,2,256]{3,2,1,0:T(2,128)S(1)}, f32[1,9,2,256]{3,2,1,0:T(2,128)S(1)}, u32[]{:S(2)}, u32[]{:S(2)}) collective-permute-start(f32[1,9,2,256]{3,2,1,0:T(2,128)S(1)} %get-tuple-element.760), channel_id=1, source_target_pairs={{0,8},{8,16},{16,24},{24,32},{32,40},{40,48},{48,56},{56,64},{64,7... | collective-permute-start | bytes 55304 | tf_op jit(solution)/shard_map/ppermute | solution.py:22
  159.9 1.9 collective-permute-start.7
  161.9 8.1 %collective-permute-start.9 = (f32[3,9,2,256]{3,1,2,0:T(8,128)S(1)}, f32[3,9,2,256]{3,1,2,0:T(8,128)S(1)}, u32[]{:S(2)}, u32[]{:S(2)}) collective-permute-start(f32[3,9,2,256]{3,1,2,0:T(8,128)S(1)} %copy.351), channel_id=1, source_target_pairs={{0,8},{8,16},{16,24},{24,32},{32,40},{40,48},{48,56},{56,64},{64,7... | collective-permute-start | bytes 165896 | tf_op jit(solution)/shard_map/ppermute | solution.py:22
  170.0 1.9 collective-permute-start.8
  172.5 0.9 stack.135
  173.5 3.4 %all-to-all-start.1 = ((f32[8,1,9,5,256]{4,1,3,2,0:T(1,128)}), f32[8,1,9,5,256]{4,1,3,2,0:T(1,128)S(1)}, u32[]{:S(2)}, u32[]{:S(2)}) async-start(f32[8,1,9,5,256]{4,1,3,2,0:T(1,128)} %stack.135), calls=%async_computation.1 | async-start | bytes 737280 | tf_op jit(solution)/shard_map/all_to_all | solution.py:151
  176.9 3.9 %collective-permute-done.8 = f32[3,9,2,256]{3,1,2,0:T(8,128)S(1)} collective-permute-done((f32[3,9,2,256]{3,1,2,0:T(8,128)S(1)}, f32[3,9,2,256]{3,1,2,0:T(8,128)S(1)}, u32[]{:S(2)}, u32[]{:S(2)}) %collective-permute-start.8) | collective-permute-done | bytes 55328 | tf_op jit(solution)/shard_map/ppermute | solution.py:23
  181.2 10.7 %all-to-all-done.1 = f32[8,1,9,5,256]{4,1,3,2,0:T(1,128)S(1)} async-done(((f32[8,1,9,5,256]{4,1,3,2,0:T(1,128)}), f32[8,1,9,5,256]{4,1,3,2,0:T(1,128)S(1)}, u32[]{:S(2)}, u32[]{:S(2)}) %all-to-all-start.1) | async-done | bytes 368672 | tf_op jit(solution)/shard_map/all_to_all | solution.py:151
  191.9 0.9 stack.136
  192.7 3.5 %all-to-all-start.2 = ((f32[8,2,9,3,256]{4,1,3,2,0:T(2,128)}), f32[8,2,9,3,256]{4,1,3,2,0:T(2,128)S(1)}, u32[]{:S(2)}, u32[]{:S(2)}) async-start(f32[8,2,9,3,256]{4,1,3,2,0:T(2,128)} %stack.136), calls=%async_computation.2 | async-start | bytes 884736 | tf_op jit(solution)/shard_map/all_to_all | solution.py:151
  197.0 15.1 %all-to-all-done.2 = f32[8,2,9,3,256]{4,1,3,2,0:T(2,128)S(1)} async-done(((f32[8,2,9,3,256]{4,1,3,2,0:T(2,128)}), f32[8,2,9,3,256]{4,1,3,2,0:T(2,128)S(1)}, u32[]{:S(2)}, u32[]{:S(2)}) %all-to-all-start.2) | async-done | bytes 442400 | tf_op jit(solution)/shard_map/all_to_all | solution.py:151
  213.1 16.8 %while.89 = (s32[]{:T(128)}, f32[8,4,4,512]{3,2,1,0:T(4,128)S(1)}, s32[8,3,512]{2,1,0:T(4,128)}, f32[8,3,512]{2,1,0:T(4,128)S(1)}, f32[108,256]{1,0:T(8,128)S(1)}, /*index=5*/s32[]{:T(128)}, s32[]{:T(128)}, s32[]{}, s32[]{}) while((s32[]{:T(128)}, f32[8,4,4,512]{3,2,1,0:T(4,128)S(1)}, s32[8,3,512]{2,1,0:T(4,128)}, ...), condition=%wide.region_18.19_spmd, body=%wide.region_13.18_spmd.sunk | while | flops 341865984 | bytes 4495505 | solution.py:110
  230.9 2.8 gather_fusion.7
  234.0 1.9 collective-permute-start.10
  235.9 8.1 %collective-permute-start.11 = (f32[6,1,256]{2,1,0:T(1,128)S(1)}, f32[6,1,256]{2,1,0:T(1,128)S(1)}, u32[]{:S(2)}, u32[]{:S(2)}) collective-permute-start(f32[6,1,256]{2,1,0:T(1,128)S(1)} %get-tuple-element.773), channel_id=1, source_target_pairs={{0,8},{8,16},{16,24},{24,32},{32,40},{40,48},{48,56},{56,64},{64,7... | collective-permute-start | bytes 18440 | tf_op jit(solution)/shard_map/ppermute | solution.py:22
  244.0 1.9 collective-permute-start.12
  246.0 2.4 collective-permute-start.13
  248.4 14.1 %gather_fusion.6 = f32[4096,6]{1,0:T(8,128)} fusion(f32[6,4096]{0,1:T(8,128)S(1)} %copy.319, s32[4096]{0:T(1024)S(1)} %get-tuple-element.778), kind=kCustom, calls=%fused_computation.6 | custom fusion | bytes 212992 | tf_op jit(solution)/shard_map/gather | solution.py:258
  262.5 3.6 %select_bitcast_fusion = f32[6,4096]{0,1:T(8,128)S(1)} fusion(f32[4096,6]{1,0:T(8,128)} %gather_fusion.6, pred[4096]{0:T(1024)(128)(4,1)S(1)} %get-tuple-element.613), kind=kLoop, calls=%fused_computation.324 | loop fusion | flops 24576 | bytes 200704 | tf_op jit(solution)/shard_map/jit(_where)/select_n | solution.py:258
  266.4 4.1 %scatter_fusion = f32[6,4096]{0,1:T(8,128)S(1)} fusion(f32[6,4096]{0,1:T(8,128)S(1)} %select_bitcast_fusion, s32[1024]{0:T(1024)S(1)} %bitcast.456, f32[1024,6]{1,0:T(8,128)S(1)} %bitcast.371), kind=kCustom, calls=%fused_computation.9 | custom fusion | bytes 77824 | tf_op jit(solution)/shard_map/scatter | solution.py:260
  270.5 2.7 fusion.252
  273.2 2.2 copy.355
  275.4 13.4 %while.94 = (s32[]{:T(128)}, f32[3,27,256]{2,1,0:T(8,128)S(1)}, f32[8,3,512]{2,1,0:T(4,128)S(1)}, s32[8,3,512]{2,1,0:T(4,128)}, f32[8,3,512]{2,1,0:T(4,128)S(1)}, /*index=5*/s32[]{:T(128)}, s32[]{:T(128)}, s32[]{}, s32[]{}) while((s32[]{:T(128)}, f32[3,27,256]{2,1,0:T(8,128)S(1)}, f32[8,3,512]{2,1,0:T(4,128)S(1)}, ...), condition=%wide.region_22.23_spmd.clone, body=%wide.region_21.22_spmd.clone.sunk | while | flops 128304640 | bytes 370843 | solution.py:80
  288.9 4.1 %collective-permute-start.15 = (f32[3,9,2,256]{3,1,2,0:T(8,128)S(1)}, f32[3,9,2,256]{3,1,2,0:T(8,128)S(1)}, u32[]{:S(2)}, u32[]{:S(2)}) collective-permute-start(f32[3,9,2,256]{3,1,2,0:T(8,128)S(1)} %copy.359), channel_id=1, source_target_pairs={{0,8},{8,16},{16,24},{24,32},{32,40},{40,48},{48,56},{56,64},{64,7... | collective-permute-start | bytes 165896 | tf_op jit(solution)/shard_map/ppermute | solution.py:22
  293.0 1.9 collective-permute-start.14
  295.0 1.0 collective-permute-done.15
  296.0 10.3 %collective-permute-done.14 = f32[3,9,2,256]{3,1,2,0:T(8,128)S(1)} collective-permute-done((f32[3,9,2,256]{3,1,2,0:T(8,128)S(1)}, f32[3,9,2,256]{3,1,2,0:T(8,128)S(1)}, u32[]{:S(2)}, u32[]{:S(2)}) %collective-permute-start.14) | collective-permute-done | bytes 55328 | tf_op jit(solution)/shard_map/ppermute | solution.py:23
  306.6 0.9 stack.143
  307.5 3.5 %all-to-all-start.3 = ((f32[8,2,9,3,256]{4,1,3,2,0:T(2,128)}), f32[8,2,9,3,256]{4,1,3,2,0:T(2,128)S(1)}, u32[]{:S(2)}, u32[]{:S(2)}) async-start(f32[8,2,9,3,256]{4,1,3,2,0:T(2,128)} %stack.143), calls=%async_computation.3 | async-start | bytes 884736 | tf_op jit(solution)/shard_map/all_to_all | solution.py:151
  311.6 14.0 %all-to-all-done.3 = f32[8,2,9,3,256]{4,1,3,2,0:T(2,128)S(1)} async-done(((f32[8,2,9,3,256]{4,1,3,2,0:T(2,128)}), f32[8,2,9,3,256]{4,1,3,2,0:T(2,128)S(1)}, u32[]{:S(2)}, u32[]{:S(2)}) %all-to-all-start.3) | async-done | bytes 442400 | tf_op jit(solution)/shard_map/all_to_all | solution.py:151
  326.5 16.8 %while.90 = (s32[]{:T(128)}, f32[8,4,4,512]{3,2,1,0:T(4,128)S(1)}, s32[8,3,512]{2,1,0:T(4,128)}, f32[8,3,512]{2,1,0:T(4,128)S(1)}, f32[108,256]{1,0:T(8,128)S(1)}, /*index=5*/s32[]{:T(128)}, s32[]{:T(128)}, s32[]{}, s32[]{}) while((s32[]{:T(128)}, f32[8,4,4,512]{3,2,1,0:T(4,128)S(1)}, s32[8,3,512]{2,1,0:T(4,128)}, ...), condition=%wide.region_28.29_spmd, body=%wide.region_23.28_spmd.sunk | while | flops 341865984 | bytes 4495505 | solution.py:110
  (658 shorter events, 103.0 us)
Async XLA Ops:
  2.4 18.1 %copy-start.3 = (s32[4096]{0:T(1024)S(1)}, s32[4096]{0:T(1024)}, u32[]{:S(2)}) copy-start(s32[4096]{0:T(1024)} %param.26) | copy-start | bytes 49156
  14.6 28.8 %collective-permute-start = (f32[1,9,2,256]{3,2,1,0:T(2,128)S(1)}, f32[1,9,2,256]{3,2,1,0:T(2,128)S(1)}, u32[]{:S(2)}, u32[]{:S(2)}) collective-permute-start(f32[1,9,2,256]{3,2,1,0:T(2,128)S(1)} %get-tuple-element.765), channel_id=1, source_target_pairs={{0,8},{8,16},{16,24},{24,32},{32,40},{40,48},{48,56},{56,64},{64,7... | collective-permute-start | bytes 55304 | tf_op jit(solution)/shard_map/ppermute | solution.py:22
  18.0 25.4 %collective-permute-start.1 = (f32[1,9,2,256]{3,2,1,0:T(2,128)S(1)}, f32[1,9,2,256]{3,2,1,0:T(2,128)S(1)}, u32[]{:S(2)}, u32[]{:S(2)}) collective-permute-start(f32[1,9,2,256]{3,2,1,0:T(2,128)S(1)} %get-tuple-element.764), channel_id=1, source_target_pairs={{8,0},{16,8},{24,16},{32,24},{40,32},{48,40},{56,48},{64,56},{72,6... | collective-permute-start | bytes 55304 | tf_op jit(solution)/shard_map/ppermute | solution.py:23
  28.7 8.4 %copy-start = (s32[4096]{0:T(1024)S(1)}, s32[4096]{0:T(1024)}, u32[]{:S(2)}) copy-start(s32[4096]{0:T(1024)} %param.27) | copy-start | bytes 49156
  37.1 18.1 %copy-start.5 = (f32[3,4096]{1,0:T(4,128)S(1)}, f32[3,4096]{1,0:T(4,128)}, u32[]{:S(2)}) copy-start(f32[3,4096]{1,0:T(4,128)} %param.29) | copy-start | bytes 147460
  44.9 25.3 %all-to-all-start = ((f32[8,1,9,5,256]{4,1,3,2,0:T(1,128)}), f32[8,1,9,5,256]{4,1,3,2,0:T(1,128)S(1)}, u32[]{:S(2)}, u32[]{:S(2)}) async-start(f32[8,1,9,5,256]{4,1,3,2,0:T(1,128)} %stack.129), calls=%async_computation | async-start | bytes 737280 | tf_op jit(solution)/shard_map/all_to_all | solution.py:151
  71.1 13.0 %copy-start.4 = (f32[3,4096]{1,0:T(4,128)S(1)}, f32[3,4096]{1,0:T(4,128)}, u32[]{:S(2)}) copy-start(f32[3,4096]{1,0:T(4,128)} %param.23) | copy-start | bytes 147460
  87.9 14.5 %collective-permute-start.5 = (f32[7,1,256]{2,1,0:T(1,128)S(1)}, f32[7,1,256]{2,1,0:T(1,128)S(1)}, u32[]{:S(2)}, u32[]{:S(2)}) collective-permute-start(f32[7,1,256]{2,1,0:T(1,128)S(1)} %get-tuple-element.768), channel_id=1, source_target_pairs={{1,0},{2,1},{3,2},{4,3},{5,4},{6,5},{7,6},{0,7},{9,8},{10,9},{11,1... | collective-permute-start | bytes 21512 | tf_op jit(solution)/shard_map/ppermute | solution.py:23
  89.8 12.6 %collective-permute-start.4 = (f32[7,1,256]{2,1,0:T(1,128)S(1)}, f32[7,1,256]{2,1,0:T(1,128)S(1)}, u32[]{:S(2)}, u32[]{:S(2)}) collective-permute-start(f32[7,1,256]{2,1,0:T(1,128)S(1)} %get-tuple-element.769), channel_id=1, source_target_pairs={{0,1},{1,2},{2,3},{3,4},{4,5},{5,6},{6,7},{7,0},{8,9},{9,10},{10,1... | collective-permute-start | bytes 21512 | tf_op jit(solution)/shard_map/ppermute | solution.py:22
  92.2 10.2 %collective-permute-start.3 = (f32[7,1,256]{2,1,0:T(1,128)S(1)}, f32[7,1,256]{2,1,0:T(1,128)S(1)}, u32[]{:S(2)}, u32[]{:S(2)}) collective-permute-start(f32[7,1,256]{2,1,0:T(1,128)S(1)} %get-tuple-element.767), channel_id=1, source_target_pairs={{8,0},{16,8},{24,16},{32,24},{40,32},{48,40},{56,48},{64,56},{72,6... | collective-permute-start | bytes 21512 | tf_op jit(solution)/shard_map/ppermute | solution.py:23
  95.5 8.1 %collective-permute-start.2 = (f32[7,1,256]{2,1,0:T(1,128)S(1)}, f32[7,1,256]{2,1,0:T(1,128)S(1)}, u32[]{:S(2)}, u32[]{:S(2)}) collective-permute-start(f32[7,1,256]{2,1,0:T(1,128)S(1)} %get-tuple-element.766), channel_id=1, source_target_pairs={{0,8},{8,16},{16,24},{24,32},{32,40},{40,48},{48,56},{56,64},{64,7... | collective-permute-start | bytes 21512 | tf_op jit(solution)/shard_map/ppermute | solution.py:22
  122.7 2.4 copy-start.2
  151.5 20.5 %collective-permute-start.6 = (f32[1,9,2,256]{3,2,1,0:T(2,128)S(1)}, f32[1,9,2,256]{3,2,1,0:T(2,128)S(1)}, u32[]{:S(2)}, u32[]{:S(2)}) collective-permute-start(f32[1,9,2,256]{3,2,1,0:T(2,128)S(1)} %get-tuple-element.760), channel_id=1, source_target_pairs={{0,8},{8,16},{16,24},{24,32},{32,40},{40,48},{48,56},{56,64},{64,7... | collective-permute-start | bytes 55304 | tf_op jit(solution)/shard_map/ppermute | solution.py:22
  159.9 12.1 %collective-permute-start.7 = (f32[1,9,2,256]{3,2,1,0:T(2,128)S(1)}, f32[1,9,2,256]{3,2,1,0:T(2,128)S(1)}, u32[]{:S(2)}, u32[]{:S(2)}) collective-permute-start(f32[1,9,2,256]{3,2,1,0:T(2,128)S(1)} %get-tuple-element.759), channel_id=1, source_target_pairs={{8,0},{16,8},{24,16},{32,24},{40,32},{48,40},{56,48},{64,56},{72,6... | collective-permute-start | bytes 55304 | tf_op jit(solution)/shard_map/ppermute | solution.py:23
  161.9 15.0 %collective-permute-start.9 = (f32[3,9,2,256]{3,1,2,0:T(8,128)S(1)}, f32[3,9,2,256]{3,1,2,0:T(8,128)S(1)}, u32[]{:S(2)}, u32[]{:S(2)}) collective-permute-start(f32[3,9,2,256]{3,1,2,0:T(8,128)S(1)} %copy.351), channel_id=1, source_target_pairs={{0,8},{8,16},{16,24},{24,32},{32,40},{40,48},{48,56},{56,64},{64,7... | collective-permute-start | bytes 165896 | tf_op jit(solution)/shard_map/ppermute | solution.py:22
  170.0 10.8 %collective-permute-start.8 = (f32[3,9,2,256]{3,1,2,0:T(8,128)S(1)}, f32[3,9,2,256]{3,1,2,0:T(8,128)S(1)}, u32[]{:S(2)}, u32[]{:S(2)}) collective-permute-start(f32[3,9,2,256]{3,1,2,0:T(8,128)S(1)} %copy.350), channel_id=1, source_target_pairs={{8,0},{16,8},{24,16},{32,24},{40,32},{48,40},{56,48},{64,56},{72,6... | collective-permute-start | bytes 165896 | tf_op jit(solution)/shard_map/ppermute | solution.py:23
  173.5 18.4 %all-to-all-start.1 = ((f32[8,1,9,5,256]{4,1,3,2,0:T(1,128)}), f32[8,1,9,5,256]{4,1,3,2,0:T(1,128)S(1)}, u32[]{:S(2)}, u32[]{:S(2)}) async-start(f32[8,1,9,5,256]{4,1,3,2,0:T(1,128)} %stack.135), calls=%async_computation.1 | async-start | bytes 737280 | tf_op jit(solution)/shard_map/all_to_all | solution.py:151
  192.7 19.4 %all-to-all-start.2 = ((f32[8,2,9,3,256]{4,1,3,2,0:T(2,128)}), f32[8,2,9,3,256]{4,1,3,2,0:T(2,128)S(1)}, u32[]{:S(2)}, u32[]{:S(2)}) async-start(f32[8,2,9,3,256]{4,1,3,2,0:T(2,128)} %stack.136), calls=%async_computation.2 | async-start | bytes 884736 | tf_op jit(solution)/shard_map/all_to_all | solution.py:151
  213.1 17.1 %copy-start.6 = (f32[3,4096]{1,0:T(4,128)S(1)}, f32[3,4096]{1,0:T(4,128)}, u32[]{:S(2)}) copy-start(f32[3,4096]{1,0:T(4,128)} %param.28) | copy-start | bytes 147460
  234.0 32.1 %collective-permute-start.10 = (f32[6,1,256]{2,1,0:T(1,128)S(1)}, f32[6,1,256]{2,1,0:T(1,128)S(1)}, u32[]{:S(2)}, u32[]{:S(2)}) collective-permute-start(f32[6,1,256]{2,1,0:T(1,128)S(1)} %get-tuple-element.770), channel_id=1, source_target_pairs={{8,0},{16,8},{24,16},{32,24},{40,32},{48,40},{56,48},{64,56},{72,6... | collective-permute-start | bytes 18440 | tf_op jit(solution)/shard_map/ppermute | solution.py:23
  235.9 30.2 %collective-permute-start.11 = (f32[6,1,256]{2,1,0:T(1,128)S(1)}, f32[6,1,256]{2,1,0:T(1,128)S(1)}, u32[]{:S(2)}, u32[]{:S(2)}) collective-permute-start(f32[6,1,256]{2,1,0:T(1,128)S(1)} %get-tuple-element.773), channel_id=1, source_target_pairs={{0,8},{8,16},{16,24},{24,32},{32,40},{40,48},{48,56},{56,64},{64,7... | collective-permute-start | bytes 18440 | tf_op jit(solution)/shard_map/ppermute | solution.py:22
  244.0 22.1 %collective-permute-start.12 = (f32[6,1,256]{2,1,0:T(1,128)S(1)}, f32[6,1,256]{2,1,0:T(1,128)S(1)}, u32[]{:S(2)}, u32[]{:S(2)}) collective-permute-start(f32[6,1,256]{2,1,0:T(1,128)S(1)} %get-tuple-element.772), channel_id=1, source_target_pairs={{1,0},{2,1},{3,2},{4,3},{5,4},{6,5},{7,6},{0,7},{9,8},{10,9},{11,1... | collective-permute-start | bytes 18440 | tf_op jit(solution)/shard_map/ppermute | solution.py:23
  246.0 20.2 %collective-permute-start.13 = (f32[6,1,256]{2,1,0:T(1,128)S(1)}, f32[6,1,256]{2,1,0:T(1,128)S(1)}, u32[]{:S(2)}, u32[]{:S(2)}) collective-permute-start(f32[6,1,256]{2,1,0:T(1,128)S(1)} %get-tuple-element.771), channel_id=1, source_target_pairs={{0,1},{1,2},{2,3},{3,4},{4,5},{5,6},{6,7},{7,0},{8,9},{9,10},{10,1... | collective-permute-start | bytes 18440 | tf_op jit(solution)/shard_map/ppermute | solution.py:22
  288.8 22.2 %copy-start.1 = (f32[3,4096]{0,1:T(8,128)S(1)}, f32[3,4096]{0,1:T(8,128)}, u32[]{:S(2)}) copy-start(f32[3,4096]{0,1:T(8,128)} %get-tuple-element.718) | copy-start | bytes 147460
  288.9 7.1 %collective-permute-start.15 = (f32[3,9,2,256]{3,1,2,0:T(8,128)S(1)}, f32[3,9,2,256]{3,1,2,0:T(8,128)S(1)}, u32[]{:S(2)}, u32[]{:S(2)}) collective-permute-start(f32[3,9,2,256]{3,1,2,0:T(8,128)S(1)} %copy.359), channel_id=1, source_target_pairs={{0,8},{8,16},{16,24},{24,32},{32,40},{40,48},{48,56},{56,64},{64,7... | collective-permute-start | bytes 165896 | tf_op jit(solution)/shard_map/ppermute | solution.py:22
  293.0 13.2 %collective-permute-start.14 = (f32[3,9,2,256]{3,1,2,0:T(8,128)S(1)}, f32[3,9,2,256]{3,1,2,0:T(8,128)S(1)}, u32[]{:S(2)}, u32[]{:S(2)}) collective-permute-start(f32[3,9,2,256]{3,1,2,0:T(8,128)S(1)} %copy.358), channel_id=1, source_target_pairs={{8,0},{16,8},{24,16},{32,24},{40,32},{48,40},{56,48},{64,56},{72,6... | collective-permute-start | bytes 165896 | tf_op jit(solution)/shard_map/ppermute | solution.py:23
  307.5 18.1 %all-to-all-start.3 = ((f32[8,2,9,3,256]{4,1,3,2,0:T(2,128)}), f32[8,2,9,3,256]{4,1,3,2,0:T(2,128)S(1)}, u32[]{:S(2)}, u32[]{:S(2)}) async-start(f32[8,2,9,3,256]{4,1,3,2,0:T(2,128)} %stack.143), calls=%async_computation.3 | async-start | bytes 884736 | tf_op jit(solution)/shard_map/all_to_all | solution.py:151
